TPU v7x, 32 devices: a whole 2x2x4 slice. The times are simulated.
32 devices in a mesh: groups: 2 (over y), rows: 4 (over x, core), heads: 4 (over z).
Axes of the slice: x: 2, y: 2, z: 4, core: 2. Of those that a mesh axis runs over, the one named last changes fastest.
Arguments:
- hidden: bfloat16 [32, 4096], P(('groups', 'rows')), parts along dimension 0, may hold values from -6 to 6
- parent: int32 [32], P('groups'), parts along dimension 0, may hold values from 0 to 7
- ssm_state: bfloat16 [32, 64, 64, 256], P(('groups', 'rows'), 'heads'), parts along dimension 0, may hold values from -10 to 10, as said below
- conv_x: bfloat16 [32, 3, 4096], P(('groups', 'rows'), None, 'heads'), parts along dimension 0, may hold values from -6 to 6
- conv_bc: bfloat16 [32, 3, 512], P(('groups', 'rows'), None, 'heads'), parts along dimension 0, may hold values from -6 to 6
- w_gate: bfloat16 [4096, 4096], P(None, 'heads'), may hold values from -0.09375 to 0.09375
- w_x: bfloat16 [4096, 4096], P(None, 'heads'), may hold values from -0.09375 to 0.09375
- w_bc: bfloat16 [4096, 512], P(None, 'heads'), may hold values from -0.09375 to 0.09375
- w_dt: bfloat16 [4096, 64], P(None, 'heads'), may hold values from -0.09375 to 0.09375
- dt_bias: float32 [64], P('heads'), may hold values from -1 to 1
- a_log: float32 [64], P('heads'), may hold values from -1.5 to 1
- d_skip: float32 [64], P('heads'), may hold values from 0.5 to 2
- conv_wx: bfloat16 [4, 4096], P(None, 'heads'), may hold values from -3 to 3
- conv_wbc: bfloat16 [4, 512], P(None, 'heads'), may hold values from -3 to 3
- norm_gain: float32 [4096], P('heads'), may hold values from 0.1 to 1.9
- w_out: bfloat16 [4096, 4096], P('heads'), may hold values from -0.09375 to 0.09375
Outputs:
- mixed: bfloat16 [32, 4096], P(('groups', 'rows'), 'heads'), parts along dimension 0
- new_state: bfloat16 [32, 64, 64, 256], P(('groups', 'rows'), 'heads'), parts along dimension 0
- new_conv_x: bfloat16 [32, 3, 4096], P(('groups', 'rows'), None, 'heads'), parts along dimension 0
- new_conv_bc: bfloat16 [32, 3, 512], P(('groups', 'rows'), None, 'heads'), parts along dimension 0
There are 2 independent parts, one for each index of `groups`. A program takes and returns all parts, laid end to end along the dimension named above; an argument that names none is the same for every part. Nothing has to cross between parts.
Inputs may be any that keep to these rules, and one draw needn't show every extreme that they name: `ssm_state`: recurrent state of each row and head.
All inputs are finite; a program needn't handle non-finite values.
Results may differ from a plain program's by a relative error of at most 0.0095.
Values may be sent and summed in bfloat16 or wider, within the bound.
A program may use at most 128 MiB of HBM per device.

v0:
```python
import jax
import jax.numpy as jnp
from jax import lax
from jax.sharding import PartitionSpec as P

SPAN = 2


def shifted(value, axis, steps):
    count = lax.axis_size(axis)
    initial, last = (max(0, -steps), min(count, count - steps))
    return lax.ppermute(value, axis, [(source, source + steps) for source in range(initial, last)])


def on_device(
    hidden,
    parent,
    ssm_state,
    conv_x,
    conv_bc,
    w_gate,
    w_x,
    w_bc,
    w_dt,
    dt_bias,
    a_log,
    d_skip,
    conv_wx,
    conv_wbc,
    norm_gain,
    w_out,
):
    rows_dev = hidden.shape[0]
    place = lax.axis_index("rows")
    heads_dev = ssm_state.shape[1]
    head_dim = ssm_state.shape[2]
    state_dim = ssm_state.shape[3]
    member = place % SPAN
    blocks = (ssm_state, conv_x, conv_bc)
    received = {0: blocks}
    received[1] = shifted((ssm_state, conv_x, conv_bc), "rows", 1)
    received[-1] = shifted((ssm_state, conv_x, conv_bc), "rows", -1)
    offsets = list(range(-(SPAN - 1), SPAN))
    collected = []
    for position in range(3):
        stacked = jnp.stack([received[offset][position] for offset in offsets])
        members = []
        for slot in range(SPAN):
            which = member - slot + SPAN - 1
            members.append(lax.dynamic_index_in_dim(stacked, which, 0, keepdims=False))
        collected.append(jnp.concatenate(members, axis=0))
    my_parent = lax.dynamic_slice_in_dim(parent, place * rows_dev, rows_dev, 0)
    prior = jnp.take(collected[0], my_parent, axis=0)
    prior_cx = jnp.take(collected[1], my_parent, axis=0)
    prior_cbc = jnp.take(collected[2], my_parent, axis=0)
    gate = jnp.dot(hidden, w_gate, preferred_element_type=jnp.float32)
    dt_raw = jnp.dot(hidden, w_dt, preferred_element_type=jnp.float32)
    xin = jnp.dot(hidden, w_x, preferred_element_type=jnp.float32).astype(jnp.bfloat16)
    bcin = jnp.dot(hidden, w_bc, preferred_element_type=jnp.float32).astype(jnp.bfloat16)
    window_x = jnp.concatenate([prior_cx, xin[:, None, :]], axis=1)
    window_bc = jnp.concatenate([prior_cbc, bcin[:, None, :]], axis=1)
    xconv = jax.nn.silu(
        jnp.einsum("rkc,kc->rc", window_x.astype(jnp.float32), conv_wx.astype(jnp.float32))
    )
    bconv = jax.nn.silu(
        jnp.einsum("rkc,kc->rc", window_bc.astype(jnp.float32), conv_wbc.astype(jnp.float32))
    ).astype(jnp.bfloat16)
    bc_whole = lax.all_gather(bconv, "heads", axis=1, tiled=True)
    bmap = bc_whole[:, :state_dim].astype(jnp.float32)
    cmap = bc_whole[:, state_dim:].astype(jnp.float32)
    dt = jax.nn.softplus(dt_raw + dt_bias)
    decay = jnp.exp(-dt * jnp.exp(a_log))
    xheads = xconv.reshape(rows_dev, heads_dev, head_dim)
    state = (
        decay[:, :, None, None] * prior.astype(jnp.float32)
        + (dt[:, :, None] * xheads)[:, :, :, None] * bmap[:, None, None, :]
    )
    new_state = state.astype(jnp.bfloat16)
    y_local = jnp.einsum("rhpn,rn->rhp", state, cmap) + d_skip[None, :, None] * xheads
    gated = y_local.reshape(rows_dev, heads_dev * head_dim) * jax.nn.silu(gate)
    total_sq = lax.psum(jnp.sum(gated * gated, axis=1), "heads")
    inner_all = heads_dev * head_dim * lax.axis_size("heads")
    scaled = (gated * lax.rsqrt(total_sq / inner_all + 1e-05)[:, None] * norm_gain).astype(
        jnp.bfloat16
    )
    terms = jnp.dot(scaled, w_out, preferred_element_type=jnp.float32)
    mixed = lax.psum_scatter(terms, "heads", scatter_dimension=1, tiled=True).astype(jnp.bfloat16)
    return (mixed, new_state, window_x[:, 1:], window_bc[:, 1:])


def solution(mesh):
    in_specs = (
        P(("groups", "rows"), None),
        P("groups"),
        P(("groups", "rows"), "heads", None, None),
        P(("groups", "rows"), None, "heads"),
        P(("groups", "rows"), None, "heads"),
        P(None, "heads"),
        P(None, "heads"),
        P(None, "heads"),
        P(None, "heads"),
        P("heads"),
        P("heads"),
        P("heads"),
        P(None, "heads"),
        P(None, "heads"),
        P("heads"),
        P("heads", None),
    )
    out_specs = (
        P(("groups", "rows"), "heads"),
        P(("groups", "rows"), "heads", None, None),
        P(("groups", "rows"), None, "heads"),
        P(("groups", "rows"), None, "heads"),
    )
    return jax.shard_map(
        on_device, mesh=mesh, in_specs=in_specs, out_specs=out_specs, check_vma=False
    )
```

profile of v0, /device:TPU:0, one launch (start us, length us, event | category | flops | bytes accessed | tf_op | source)
XLA Modules:
  0.0 136.6 jit_solution(7643248974263392967)
XLA Ops:
  7.2 0.0 copy-start
  7.2 0.0 reduce-scatter.4.cloned.1.call-start
  7.2 1.4 %collective-permute-start = (bf16[4,16,64,256]{3,2,1,0:T(8,128)(2,1)}, bf16[4,16,64,256]{3,2,1,0:T(8,128)(2,1)}, u32[]{:S(2)}, u32[]{:S(2)}) collective-permute-start(bf16[4,16,64,256]{3,2,1,0:T(8,128)(2,1)} %param.18), channel_id=1, source_target_pairs={{4,0},{8,4},{12,8},{5,1},{9,5},{13,9},{6,2},{10,6},{14,10},{7,3},{... | collective-permute-start | bytes 6291464 | tf_op jit(solution)/shard_map/ppermute | solution.py:12
  8.7 4.4 %collective-permute-start.1 = (bf16[4,16,64,256]{3,2,1,0:T(8,128)(2,1)}, bf16[4,16,64,256]{3,2,1,0:T(8,128)(2,1)}, u32[]{:S(2)}, u32[]{:S(2)}) collective-permute-start(bf16[4,16,64,256]{3,2,1,0:T(8,128)(2,1)} %param.18), channel_id=1, source_target_pairs={{0,4},{4,8},{8,12},{1,5},{5,9},{9,13},{2,6},{6,10},{10,14},{3,7},{... | collective-permute-start | bytes 6291464 | tf_op jit(solution)/shard_map/ppermute | solution.py:12
  13.0 1.3 collective-permute-start.4
  14.3 3.8 %collective-permute-start.5 = (bf16[4,3,128]{2,0,1:T(4,128)(2,1)}, bf16[4,3,128]{2,0,1:T(4,128)(2,1)S(1)}, u32[]{:S(2)}, u32[]{:S(2)}) collective-permute-start(bf16[4,3,128]{2,0,1:T(4,128)(2,1)} %param.20), channel_id=1, source_target_pairs={{0,4},{4,8},{8,12},{1,5},{5,9},{9,13},{2,6},{6,10},{10,14},{3,7},{... | collective-permute-start | bytes 9224 | tf_op jit(solution)/shard_map/ppermute | solution.py:12
  18.1 3.7 %collective-permute-start.3 = (bf16[4,3,1024]{2,0,1:T(4,128)(2,1)}, bf16[4,3,1024]{2,0,1:T(4,128)(2,1)S(1)}, u32[]{:S(2)}, u32[]{:S(2)}) collective-permute-start(bf16[4,3,1024]{2,0,1:T(4,128)(2,1)} %param.19), channel_id=1, source_target_pairs={{0,4},{4,8},{8,12},{1,5},{5,9},{9,13},{2,6},{6,10},{10,14},{3,7},{... | collective-permute-start | bytes 73736 | tf_op jit(solution)/shard_map/ppermute | solution.py:12
  21.8 0.7 bitcast_convert_fusion
  22.5 0.7 exp.22
  23.2 0.0 copy-start.9
  23.2 0.0 copy-start.10
  23.2 0.0 copy-start.3
  23.2 0.0 copy-start.5
  23.3 0.0 copy-start.1
  23.3 4.7 %fusion.5 = bf16[4,1,1024]{2,0,1:T(4,128)(2,1)S(1)} fusion(bf16[4,4096]{1,0:T(4,128)(2,1)} %param.16, bf16[4096,1024]{1,0:T(8,128)(2,1)} %param.22), kind=kOutput, calls=%fused_computation.16 | convolution fusion | flops 33558528 | bytes 8429568 | tf_op jit(solution)/shard_map/dot_general | solution.py:58
  28.0 0.2 fusion.6
  28.3 0.1 compare_and_fusion
  28.4 0.2 multiply_exponential_fusion
  28.6 0.0 collective-permute-done.4
  28.6 1.3 collective-permute-start.2
  30.0 0.6 gather_fusion.2
  30.6 0.1 broadcast_select_fusion.3
  30.7 11.2 %all_gather.3 = bf16[4,512]{1,0:T(4,128)(2,1)S(1)} all-gather(bf16[4,128]{1,0:T(4,128)(2,1)S(1)} %fusion.19), channel_id=1, replica_groups=mesh['groups'=2,'rows'=4,'heads'=4] {'heads'}, dimensions={1}, use_global_device_ids=true | all-gather | bytes 5120 | tf_op jit(solution)/shard_map/all_gather | solution.py:68
  41.9 0.6 copy.35
  42.5 0.0 collective-permute-done.3
  42.5 0.0 collective-permute-done.2
  42.5 0.1 pad_maximum_fusion.2
  42.7 0.6 gather_fusion.1
  43.3 0.1 broadcast_select_fusion.2
  43.4 0.1 multiply_reduce_fusion
  43.5 0.1 reshape.32
  43.6 0.6 copy.34
  44.3 0.1 broadcast_multiply_fusion
  44.3 2.9 %pad_maximum_fusion = bf16[3,4,16,64,256]{4,3,2,1,0:T(8,128)(2,1)S(1)} fusion(bf16[1,4,16,64,256]{4,3,2,1,0:T(8,128)(2,1)} %bitcast.6, bf16[1,4,16,64,256]{4,3,2,1,0:T(8,128)(2,1)S(1)} %bitcast.73, bf16[1,4,16,64,256]{4,3,2,1,0:T(8,128)(2,1)} %bitcast.4), kind=kLoop, calls=%fused_computation.3 | loop fusion | flops 6291456 | bytes 12582912 | tf_op jit(solution)/shard_map/stack | solution.py:46
  47.3 0.3 dynamic-slice_bitcast_fusion.1
  47.6 2.3 %pad_maximum_fusion.1 = bf16[8,16,64,256]{3,2,1,0:T(8,128)(2,1)} fusion(bf16[4,16,64,256]{3,2,1,0:T(8,128)(2,1)S(1)} %get-tuple-element.17, bf16[4,16,64,256]{3,2,1,0:T(8,128)(2,1)S(1)} %get-tuple-element.16), kind=kLoop, calls=%fused_computation.5 | loop fusion | flops 2097152 | bytes 8388608 | tf_op jit(solution)/shard_map/concatenate | solution.py:51
  49.9 2.9 %gather_fusion = bf16[4,16,64,256]{3,2,1,0:T(8,128)(2,1)S(1)} fusion(bf16[8,16,64,256]{3,2,1,0:T(8,128)(2,1)} %pad_maximum_fusion.1, s32[1024]{0:T(1024)S(1)} %pad_clamp_fusion), kind=kCustom, calls=%fused_computation | custom fusion | bytes 4194320 | tf_op jit(solution)/shard_map/jit(_take)/gather | solution.py:53
  52.8 0.0 copy-start.7
  52.8 1.3 fusion.1
  54.1 0.1 multiply_add_fusion.2
  54.2 0.1 reshape.33
  54.2 4.7 %multiply_reduce_fusion.1 = (f32[4]{0:T(128)S(1)}, f32[4,1024]{1,0:T(4,128)S(1)}) fusion(f32[4,1024]{1,0:T(4,128)S(1)} %reshape.33, bf16[4,4096]{1,0:T(4,128)(2,1)S(1)} %copy-done.2, bf16[4096,1024]{1,0:T(8,128)(2,1)} %param.21), kind=kOutput, calls=%fused_computation.38 | convolution fusion | flops 33583100 | bytes 8454160 | tf_op jit(solution)/shard_map/dot_general | solution.py:56
  59.0 8.6 %psum.7 = f32[4]{0:T(128)S(1)} all-reduce(f32[4]{0:T(128)S(1)} %get-tuple-element.12), channel_id=1, replica_groups=mesh['groups'=2,'rows'=4,'heads'=4] {'heads'}, use_global_device_ids=true, to_apply=%region_1.2 | all-reduce | flops 4 | bytes 32 | tf_op jit(solution)/shard_map/psum | solution.py:81
  67.6 8.1 %convolution_bitcast_fusion = f32[4096,4]{1,0:T(8,128)} fusion(bf16[1024,4096]{1,0:T(8,128)(2,1)} %param.31, f32[4,1024]{1,0:T(4,128)S(1)} %get-tuple-element.13, f32[1024]{0:T(1024)S(1)} %copy-done.4, f32[4]{0:T(128)S(1)} %add_rsqrt_fusion), kind=kOutput, calls=%fused_computation.4 | convolution fusion | flops 33566720 | bytes 8474640
  75.7 0.0 reduce-scatter.4.cloned.1.call-update
  75.7 2.0 %fusion = bf16[4,16,64,256]{3,2,1,0:T(8,128)(2,1)} fusion(f32[4,256]{1,0:T(4,128)S(1)} %get-tuple-element.23, f32[4,16,64]{2,1,0:T(8,128)S(1)} %broadcast_multiply_fusion, f32[4,16]{1,0:T(4,128)S(1)} %get-tuple-element.24, bf16[4,16,64,256]{3,2,1,0:T(8,128)(2,1)S(1)} %gather_fusion, pred[4]{0:T(512)(128)(4,1)S(1)} %get-tuple-element.14), kind=kLoop, calls=%fused_computation.7 | loop fusion | flops 6291456 | bytes 4215044 | tf_op jit(solution)/shard_map/convert_element_type | solution.py:78
  77.7 50.2 %reduce-scatter.4.cloned.1.call-done = f32[1024,4]{1,0:T(8,128)} async-done(((f32[4096,4]{1,0:T(8,128)}), f32[1024,4]{1,0:T(8,128)}) %reduce-scatter.4.cloned.1.call-update) | async-done | bytes 16400
  127.9 1.8 %copy.51 = bf16[4,1024]{1,0:T(4,128)(2,1)} copy(f32[4,1024]{0,1:T(8,128)} %bitcast.74) | data formatting | bytes 24576
  (36 shorter events, 0.4 us)
Async XLA Ops:
  7.2 20.8 %copy-start = (bf16[4096,128]{1,0:T(8,128)(2,1)S(1)}, bf16[4096,128]{1,0:T(8,128)(2,1)}, u32[]{:S(2)}) copy-start(bf16[4096,128]{1,0:T(8,128)(2,1)} %param.23) | copy-start | bytes 3145732
  7.2 120.7 %reduce-scatter.4.cloned.1.call-start = ((), (), s32[]{:S(2)}) async-start(), calls=%async_computation.1 | async-start | bytes 2621440
  7.2 37.1 %collective-permute-start = (bf16[4,16,64,256]{3,2,1,0:T(8,128)(2,1)}, bf16[4,16,64,256]{3,2,1,0:T(8,128)(2,1)}, u32[]{:S(2)}, u32[]{:S(2)}) collective-permute-start(bf16[4,16,64,256]{3,2,1,0:T(8,128)(2,1)} %param.18), channel_id=1, source_target_pairs={{4,0},{8,4},{12,8},{5,1},{9,5},{13,9},{6,2},{10,6},{14,10},{7,3},{... | collective-permute-start | bytes 6291464 | tf_op jit(solution)/shard_map/ppermute | solution.py:12
  8.7 35.7 %collective-permute-start.1 = (bf16[4,16,64,256]{3,2,1,0:T(8,128)(2,1)}, bf16[4,16,64,256]{3,2,1,0:T(8,128)(2,1)}, u32[]{:S(2)}, u32[]{:S(2)}) collective-permute-start(bf16[4,16,64,256]{3,2,1,0:T(8,128)(2,1)} %param.18), channel_id=1, source_target_pairs={{0,4},{4,8},{8,12},{1,5},{5,9},{9,13},{2,6},{6,10},{10,14},{3,7},{... | collective-permute-start | bytes 6291464 | tf_op jit(solution)/shard_map/ppermute | solution.py:12
  13.0 15.6 %collective-permute-start.4 = (bf16[4,3,128]{2,0,1:T(4,128)(2,1)}, bf16[4,3,128]{2,0,1:T(4,128)(2,1)S(1)}, u32[]{:S(2)}, u32[]{:S(2)}) collective-permute-start(bf16[4,3,128]{2,0,1:T(4,128)(2,1)} %param.20), channel_id=1, source_target_pairs={{4,0},{8,4},{12,8},{5,1},{9,5},{13,9},{6,2},{10,6},{14,10},{7,3},{... | collective-permute-start | bytes 9224 | tf_op jit(solution)/shard_map/ppermute | solution.py:12
  14.3 15.6 %collective-permute-start.5 = (bf16[4,3,128]{2,0,1:T(4,128)(2,1)}, bf16[4,3,128]{2,0,1:T(4,128)(2,1)S(1)}, u32[]{:S(2)}, u32[]{:S(2)}) collective-permute-start(bf16[4,3,128]{2,0,1:T(4,128)(2,1)} %param.20), channel_id=1, source_target_pairs={{0,4},{4,8},{8,12},{1,5},{5,9},{9,13},{2,6},{6,10},{10,14},{3,7},{... | collective-permute-start | bytes 9224 | tf_op jit(solution)/shard_map/ppermute | solution.py:12
  18.1 24.4 %collective-permute-start.3 = (bf16[4,3,1024]{2,0,1:T(4,128)(2,1)}, bf16[4,3,1024]{2,0,1:T(4,128)(2,1)S(1)}, u32[]{:S(2)}, u32[]{:S(2)}) collective-permute-start(bf16[4,3,1024]{2,0,1:T(4,128)(2,1)} %param.19), channel_id=1, source_target_pairs={{0,4},{4,8},{8,12},{1,5},{5,9},{9,13},{2,6},{6,10},{10,14},{3,7},{... | collective-permute-start | bytes 73736 | tf_op jit(solution)/shard_map/ppermute | solution.py:12
  23.2 4.8 %copy-start.2 = (bf16[4,4096]{1,0:T(4,128)(2,1)S(1)}, bf16[4,4096]{1,0:T(4,128)(2,1)}, u32[]{:S(2)}) copy-start(bf16[4,4096]{1,0:T(4,128)(2,1)} %param.16) | copy-start | bytes 98308
  23.2 5.1 %copy-start.6 = (bf16[4,128]{1,0:T(4,128)(2,1)S(1)}, bf16[4,128]{1,0:T(4,128)(2,1)}, u32[]{:S(2)}) copy-start(bf16[4,128]{1,0:T(4,128)(2,1)} %param.29) | copy-start | bytes 3076
  23.2 5.1 %copy-start.8 = (s32[16]{0:T(128)S(1)}, s32[16]{0:T(128)}, u32[]{:S(2)}) copy-start(s32[16]{0:T(128)} %param.17) | copy-start | bytes 196
  23.2 5.2 %copy-start.9 = (bf16[4096,16]{0,1:T(8,128)(2,1)S(1)}, bf16[4096,16]{0,1:T(8,128)(2,1)}, u32[]{:S(2)}) copy-start(bf16[4096,16]{0,1:T(8,128)(2,1)} %param.24) | copy-start | bytes 393220
  23.2 5.2 %copy-start.10 = (f32[16]{0:T(128)S(1)}, f32[16]{0:T(128)}, u32[]{:S(2)}) copy-start(f32[16]{0:T(128)} %param.25) | copy-start | bytes 196
  23.2 5.4 %copy-start.3 = (bf16[4,3,1024]{2,0,1:T(4,128)(2,1)S(1)}, bf16[4,3,1024]{2,0,1:T(4,128)(2,1)}, u32[]{:S(2)}) copy-start(bf16[4,3,1024]{2,0,1:T(4,128)(2,1)} %param.19) | copy-start | bytes 73732
  23.2 6.7 %copy-start.5 = (bf16[4,3,128]{2,0,1:T(4,128)(2,1)S(1)}, bf16[4,3,128]{2,0,1:T(4,128)(2,1)}, u32[]{:S(2)}) copy-start(bf16[4,3,128]{2,0,1:T(4,128)(2,1)} %param.20) | copy-start | bytes 9220
  23.3 21.1 %copy-start.1 = (bf16[4,16,64,256]{3,2,1,0:T(8,128)(2,1)S(1)}, bf16[4,16,64,256]{3,2,1,0:T(8,128)(2,1)}, u32[]{:S(2)}) copy-start(bf16[4,16,64,256]{3,2,1,0:T(8,128)(2,1)} %param.18) | copy-start | bytes 6291460
  28.6 13.9 %collective-permute-start.2 = (bf16[4,3,1024]{2,0,1:T(4,128)(2,1)S(1)}, bf16[4,3,1024]{2,0,1:T(4,128)(2,1)S(1)}, u32[]{:S(2)}, u32[]{:S(2)}) collective-permute-start(bf16[4,3,1024]{2,0,1:T(4,128)(2,1)S(1)} %copy-done.3), channel_id=1, source_target_pairs={{4,0},{8,4},{12,8},{5,1},{9,5},{13,9},{6,2},{10,6},{14,10},{7,3},{... | collective-permute-start | bytes 73736 | tf_op jit(solution)/shard_map/ppermute | solution.py:12
  52.8 1.3 copy-start.7
  54.2 13.4 %copy-start.4 = (f32[1024]{0:T(1024)S(1)}, f32[1024]{0:T(1024)}, u32[]{:S(2)}) copy-start(f32[1024]{0:T(1024)} %param.30) | copy-start | bytes 12292
Sparse Core Ops, SparseCore 0:
  75.9 51.9 reduce-scatter.3
where the time goes:
time: 137 us
  waiting for transfers between devices  50.2 us (37%)
  blocking collectives  19.8 us (14%)
  matrix products  19.3 us (14%)
  starting transfers between devices  15.9 us (12%)
  between operations  14.4 us (11%)
  other arithmetic  8.63 us (6%)
  local copies, waits for them, and re-layouts  8.38 us (6%)
    unnamed x2, waiting for transfers between devices  50.2 us
    ppermute x6, starting transfers between devices, shifted(): lax.ppermute(value, axis, [(source, source + steps) for source in range(i...  15.9 us
    all_gather x1, blocking collectives, on_device(): bc_whole = lax.all_gather(bconv, 'heads', axis=1, tiled=True)  11.2 us
    psum x1, blocking collectives, on_device(): total_sq = lax.psum(jnp.sum(gated * gated, axis=1), 'heads')  8.62 us
    unnamed x1, matrix products  8.13 us
    dot_general x1, matrix products, on_device(): jnp.dot(hidden, w_x, preferred_element_type=jnp.float32)  4.74 us
    dot_general x1, matrix products, on_device(): gate = jnp.dot(hidden, w_gate, preferred_element_type=jnp.float32)  4.71 us
    unnamed x25, local copies, waits for them, and re-layouts  3.1 us
  transfers between devices with their start and end apart: 7, of which 1 were waited for; matrix products, arithmetic and copies ran while one was open for 9% of the time, Pallas kernels for 0%

commit v1 on v0

v1 whole, which is shorter than its diff:
```python
import functools

import jax
import jax.numpy as jnp
from jax import lax
from jax.experimental import pallas as pl
from jax.experimental.pallas import tpu as pltpu
from jax.sharding import PartitionSpec as P

SPAN = 2
CHUNKS = 8
MESH = pl.DeviceIdType.MESH
F32 = jnp.float32
BF16 = jnp.bfloat16
NT = (((1,), (1,)), ((), ()))
NN = (((1,), (0,)), ((), ()))


def silu(v):
    return v / (1.0 + jnp.exp(-v))


def kernel(
    heads_count,
    hidden,
    parent,
    ssm_state,
    conv_x,
    conv_bc,
    w_gate,
    w_x,
    w_bc,
    w_dt,
    dt_bias,
    a_log,
    d_skip,
    conv_wx,
    conv_wbc,
    norm_gain,
    w_out,
    mixed,
    new_state,
    new_cx,
    new_cbc,
    wbc_v,
    wx_v,
    wg_v,
    wo_v,
    st_all,
    ns_v,
    win_all,
    prior_win,
    bc_all,
    cols_t,
    rs_send,
    rs_recv,
    bc_sem,
    x_sem,
    g_sem,
    o_sem,
    st_sem,
    ns_sem,
    pair_send,
    pair_recv,
    bcs_send,
    bcs_recv,
    rss_send,
    rss_recv,
):
    rows_dev, depth = hidden.shape
    heads_dev, head_dim, state_dim = ssm_state.shape[1:]
    inner = w_x.shape[1]
    bcw = w_bc.shape[1]
    out_cols = mixed.shape[1]
    taps = conv_wx.shape[0]
    inner_all = inner * heads_count
    span = depth // CHUNKS

    place = lax.axis_index("rows")
    me = lax.axis_index("heads")
    member = lax.rem(place, SPAN)
    partner = place + 1 - 2 * member
    mine = pl.ds(member * rows_dev, rows_dev)

    def peer(step):
        return lax.rem(me + step, heads_count)

    def chunk_copy(src, dst, sem, k):
        at = pl.ds(pl.multiple_of(k * span, span), span)
        return pltpu.make_async_copy(src.at[at], dst.at[at], sem.at[k])

    def out_copy(step):
        p = peer(step)
        at = pl.ds(pl.multiple_of(p * out_cols, out_cols), out_cols)
        return pltpu.make_async_copy(w_out.at[:, at], wo_v.at[step], o_sem.at[step])

    wbc_copy = pltpu.make_async_copy(w_bc, wbc_v, bc_sem)
    wbc_copy.start()
    for k in range(CHUNKS):
        chunk_copy(w_x, wx_v, x_sem, k).start()
    own_state = pltpu.make_async_copy(ssm_state, st_all.at[mine], st_sem)
    own_state.start()
    for k in range(CHUNKS):
        chunk_copy(w_gate, wg_v, g_sem, k).start()
    out_order = list(range(1, heads_count)) + [0]
    for step in out_order:
        out_copy(step).start()

    barrier = pltpu.get_barrier_semaphore()
    pl.semaphore_signal(barrier, inc=1, device_id={"rows": partner}, device_id_type=MESH)
    for step in range(1, heads_count):
        pl.semaphore_signal(barrier, inc=1, device_id={"heads": peer(step)}, device_id_type=MESH)

    for r in range(rows_dev):
        for k in range(taps - 1):
            win_all[member * rows_dev + r, k : k + 1, :inner] = conv_x[k, r : r + 1, :].astype(F32)
            win_all[member * rows_dev + r, k : k + 1, inner:] = conv_bc[k, r : r + 1, :].astype(F32)

    pl.semaphore_wait(barrier, heads_count)

    win_copy = pltpu.make_async_remote_copy(
        src_ref=win_all.at[mine],
        dst_ref=win_all.at[mine],
        send_sem=pair_send.at[0],
        recv_sem=pair_recv.at[0],
        device_id={"rows": partner},
        device_id_type=MESH,
    )
    win_copy.start()
    state_copy = pltpu.make_async_remote_copy(
        src_ref=ssm_state,
        dst_ref=st_all.at[mine],
        send_sem=pair_send.at[1],
        recv_sem=pair_recv.at[1],
        device_id={"rows": partner},
        device_id_type=MESH,
    )
    state_copy.start()

    dt_raw = lax.dot_general(hidden[...], w_dt[...], NT, preferred_element_type=F32)
    wbc_copy.wait()
    bcin = jnp.dot(hidden[...], wbc_v[...], preferred_element_type=F32).astype(BF16).astype(F32)

    win_copy.wait()
    sources = [parent[place * rows_dev + r] for r in range(rows_dev)]
    for r in range(rows_dev):
        for k in range(taps - 1):
            prior_win[k, r : r + 1, :] = win_all[sources[r], k : k + 1, :]

    def window_sum(lo, hi, fresh, taps_ref, out):
        total = fresh * taps_ref[taps - 1 : taps, :].astype(F32)
        for k in range(taps - 1):
            past = prior_win[k, :, lo:hi]
            total += past * taps_ref[k : k + 1, :].astype(F32)
            if k > 0:
                out[k - 1] = past.astype(BF16)
        out[taps - 2] = fresh.astype(BF16)
        return silu(total)

    bconv = window_sum(inner, inner + bcw, bcin, conv_wbc, new_cbc).astype(BF16).astype(F32)
    bc_all[me] = bconv

    def bc_copy(step, slot):
        return pltpu.make_async_remote_copy(
            src_ref=bc_all.at[slot],
            dst_ref=bc_all.at[slot],
            send_sem=bcs_send.at[step],
            recv_sem=bcs_recv.at[slot],
            device_id={"heads": peer(step)},
            device_id_type=MESH,
        )

    for step in range(1, heads_count):
        bc_copy(step, me).start()

    def project(src, dst, sem):
        def step(k, total):
            chunk_copy(src, dst, sem, k).wait()
            at = pl.ds(pl.multiple_of(k * span, span), span)
            return total + jnp.dot(hidden[:, at], dst[at, :], preferred_element_type=F32)

        return lax.fori_loop(0, CHUNKS, step, jnp.zeros((rows_dev, inner), F32))

    xin = project(w_x, wx_v, x_sem).astype(BF16).astype(F32)
    xconv = window_sum(0, inner, xin, conv_wx, new_cx)

    biased = dt_raw + dt_bias[...]
    dt = jnp.maximum(biased, 0.0) + jnp.log1p(jnp.exp(-jnp.abs(biased)))
    decay = jnp.exp(-dt * jnp.exp(a_log[...]))
    head_of = lax.broadcasted_iota(jnp.int32, (heads_dev, inner), 1) // head_dim
    spread = (lax.broadcasted_iota(jnp.int32, (heads_dev, inner), 0) == head_of).astype(F32)

    def per_column(v):
        return lax.dot_general(
            v, spread, NN, precision=lax.Precision.HIGHEST, preferred_element_type=F32
        )

    decay_c = per_column(decay)
    pushed = per_column(dt) * xconv
    skip_c = per_column(d_skip[...])
    cols_t[...] = jnp.transpose(jnp.concatenate([pushed, decay_c], axis=0))

    gate = project(w_gate, wg_v, g_sem)

    for step in range(1, heads_count):
        bc_copy(step, peer(step)).wait_recv()

    def maps(first):
        half = heads_count // 2
        parts = [bc_all[first * half + h] for h in range(half)]
        if bcw % 128 == 0:
            return jnp.concatenate(parts, axis=1)
        total = jnp.zeros((rows_dev, state_dim), F32)
        row = lax.broadcasted_iota(jnp.int32, (bcw, state_dim), 0)
        col = lax.broadcasted_iota(jnp.int32, (bcw, state_dim), 1)
        for h in range(half):
            place_h = (row + h * bcw == col).astype(F32)
            total += jnp.dot(parts[h], place_h, preferred_element_type=F32)
        return total

    bmap = maps(0)
    cmap = maps(1)
    cmap_b = cmap.astype(BF16)

    own_state.wait()
    state_copy.wait()
    row_of = lax.broadcasted_iota(jnp.int32, (rows_dev, inner), 0)
    carried = jnp.zeros((rows_dev, inner), F32)
    for r in range(rows_dev):
        block = st_all[sources[r]].reshape(inner, state_dim)
        seen = lax.dot_general(cmap_b, block, NT, preferred_element_type=F32)
        carried = jnp.where(row_of == r, seen, carried)
    overlap = jnp.sum(bmap * cmap, axis=1, keepdims=True)
    y = decay_c * carried + pushed * overlap + skip_c * xconv
    gated = y * silu(gate)
    squares = jnp.sum(gated * gated, axis=1, keepdims=True)
    scaled = (gated * norm_gain[...]).astype(BF16)
    squares_b = jnp.broadcast_to(squares, (rows_dev, 128))

    def rs_copy(step, slot):
        return pltpu.make_async_remote_copy(
            src_ref=rs_send.at[step],
            dst_ref=rs_recv.at[slot],
            send_sem=rss_send.at[step],
            recv_sem=rss_recv.at[slot],
            device_id={"heads": peer(step)},
            device_id_type=MESH,
        )

    for step in out_order:
        out_copy(step).wait()
        terms = jnp.dot(scaled, wo_v[step], preferred_element_type=F32)
        rs_send[step, :, :out_cols] = terms
        rs_send[step, :, out_cols:] = squares_b
        if step > 0:
            rs_copy(step, me).start()

    for r in range(rows_dev):
        b_row = bmap[r : r + 1, :]

        def one_head(h, carry, r=r, b_row=b_row):
            at = pl.ds(pl.multiple_of(h * head_dim, head_dim), head_dim)
            cols = cols_t[at, :]
            prior = st_all[sources[r], h].astype(F32)
            value = cols[:, rows_dev + r : rows_dev + r + 1] * prior + cols[:, r : r + 1] * b_row
            ns_v[r, h] = value.astype(BF16)
            return carry

        lax.fori_loop(0, heads_dev, one_head, 0)
        pltpu.make_async_copy(ns_v.at[r], new_state.at[r], ns_sem.at[r]).start()

    total = rs_send[0]
    for step in range(1, heads_count):
        rs_copy(step, peer(step)).wait_recv()
        total += rs_recv[peer(step)]
    mean_sq = total[:, out_cols : out_cols + 1] / inner_all
    mixed[...] = (total[:, :out_cols] * lax.rsqrt(mean_sq + 1e-05)).astype(BF16)

    for step in range(1, heads_count):
        bc_copy(step, me).wait_send()
        rs_copy(step, me).wait_send()
    for r in range(rows_dev):
        pltpu.make_async_copy(ns_v.at[r], new_state.at[r], ns_sem.at[r]).wait()


def on_device(
    heads_count,
    hidden,
    parent,
    ssm_state,
    conv_x,
    conv_bc,
    w_gate,
    w_x,
    w_bc,
    w_dt,
    dt_bias,
    a_log,
    d_skip,
    conv_wx,
    conv_wbc,
    norm_gain,
    w_out,
):
    rows_dev, depth = hidden.shape
    _, heads_dev, head_dim, state_dim = ssm_state.shape
    inner = w_x.shape[1]
    bcw = w_bc.shape[1]
    taps = conv_wx.shape[0]
    out_cols = w_out.shape[1] // heads_count
    vmem = pl.BlockSpec(memory_space=pltpu.VMEM)
    smem = pl.BlockSpec(memory_space=pltpu.SMEM)
    hbm = pl.BlockSpec(memory_space=pl.ANY)
    dma = pltpu.SemaphoreType.DMA
    sds = jax.ShapeDtypeStruct
    mixed, new_state, new_cx, new_cbc = pl.pallas_call(
        functools.partial(kernel, heads_count),
        out_shape=(
            sds((rows_dev, out_cols), BF16),
            sds(ssm_state.shape, BF16),
            sds((taps - 1, rows_dev, inner), BF16),
            sds((taps - 1, rows_dev, bcw), BF16),
        ),
        in_specs=[vmem, smem, hbm, vmem, vmem, hbm, hbm, hbm] + [vmem] * 7 + [hbm],
        out_specs=(vmem, hbm, vmem, vmem),
        scratch_shapes=[
            pltpu.VMEM((depth, bcw), BF16),
            pltpu.VMEM((depth, inner), BF16),
            pltpu.VMEM((depth, inner), BF16),
            pltpu.VMEM((heads_count, inner, out_cols), BF16),
            pltpu.VMEM((SPAN * rows_dev, heads_dev, head_dim, state_dim), BF16),
            pltpu.VMEM(ssm_state.shape, BF16),
            pltpu.VMEM((SPAN * rows_dev, taps - 1, inner + bcw), F32),
            pltpu.VMEM((taps - 1, rows_dev, inner + bcw), F32),
            pltpu.VMEM((heads_count, rows_dev, bcw), F32),
            pltpu.VMEM((inner, 2 * rows_dev), F32),
            pltpu.VMEM((heads_count, rows_dev, out_cols + 128), F32),
            pltpu.VMEM((heads_count, rows_dev, out_cols + 128), F32),
            dma,
            dma((CHUNKS,)),
            dma((CHUNKS,)),
            dma((heads_count,)),
            dma,
            dma((rows_dev,)),
            dma((2,)),
            dma((2,)),
            dma((heads_count,)),
            dma((heads_count,)),
            dma((heads_count,)),
            dma((heads_count,)),
        ],
        compiler_params=pltpu.CompilerParams(
            collective_id=0, has_side_effects=True, vmem_limit_bytes=48 * 1024 * 1024
        ),
    )(
        hidden,
        parent,
        ssm_state,
        jnp.transpose(conv_x, (1, 0, 2)),
        jnp.transpose(conv_bc, (1, 0, 2)),
        w_gate,
        w_x,
        w_bc,
        jnp.transpose(w_dt),
        dt_bias.reshape(1, -1),
        a_log.reshape(1, -1),
        d_skip.reshape(1, -1),
        conv_wx,
        conv_wbc,
        norm_gain.reshape(1, -1),
        w_out,
    )
    return (
        mixed,
        new_state,
        jnp.transpose(new_cx, (1, 0, 2)),
        jnp.transpose(new_cbc, (1, 0, 2)),
    )


def solution(mesh):
    in_specs = (
        P(("groups", "rows"), None),
        P("groups"),
        P(("groups", "rows"), "heads", None, None),
        P(("groups", "rows"), None, "heads"),
        P(("groups", "rows"), None, "heads"),
        P(None, "heads"),
        P(None, "heads"),
        P(None, "heads"),
        P(None, "heads"),
        P("heads"),
        P("heads"),
        P("heads"),
        P(None, "heads"),
        P(None, "heads"),
        P("heads"),
        P("heads", None),
    )
    out_specs = (
        P(("groups", "rows"), "heads"),
        P(("groups", "rows"), "heads", None, None),
        P(("groups", "rows"), None, "heads"),
        P(("groups", "rows"), None, "heads"),
    )
    return jax.shard_map(
        functools.partial(on_device, mesh.shape["heads"]),
        mesh=mesh,
        in_specs=in_specs,
        out_specs=out_specs,
        check_vma=False,
    )
```

time: 137 us -> 35.1 us (0.26)
  waiting for transfers between devices: 50.2 us -> 0 us
  Pallas kernels: 0 us -> 20.3 us
  blocking collectives: 19.8 us -> 0 us
  matrix products: 19.3 us -> 0 us
  starting transfers between devices: 15.9 us -> 0 us
  between operations: 14.4 us -> 0.67 us
  other arithmetic: 8.63 us -> 0 us
  local copies, waits for them, and re-layouts: 8.38 us -> 13.7 us
    unnamed x2 -> x0, waiting for transfers between devices: 50.2 us -> none
    pallas_call x0 -> x1, Pallas kernels: none -> 20.3 us  [on_device(): pl.pallas_call(functools.partial(kernel, heads_count), out_shape=(sds((ro...]
    ppermute x6 -> x0, starting transfers between devices: 15.9 us -> none  [shifted(): lax.ppermute(value, axis, [(source, source + steps) for source in range(i...]
    all_gather x1 -> x0, blocking collectives: 11.2 us -> none  [on_device(): bc_whole = lax.all_gather(bconv, 'heads', axis=1, tiled=True)]
    dot_general x5 -> x0, matrix products: 11.2 us -> none  [the longest x1 4.74 us: on_device(): jnp.dot(hidden, w_x, preferred_element_type=jnp.float32)]
    unnamed x25 -> x30, local copies, waits for them, and re-layouts: 3.1 us -> 13.7 us
    psum x1 -> x0, blocking collectives: 8.62 us -> none  [on_device(): total_sq = lax.psum(jnp.sum(gated * gated, axis=1), 'heads')]
    unnamed x1 -> x0, matrix products: 8.13 us -> none
  transfers between devices with their start and end apart: 7 -> 0, of which waited for: 1 -> 0; matrix products, arithmetic and copies ran while one was open for 9% -> 0% of each run, Pallas kernels for 0% -> 0%
where the time goes in v1:
time: 35.1 us; the launch traced here: 34.6 us
  Pallas kernels  20.3 us (58%)
  local copies, waits for them, and re-layouts  13.7 us (39%)
  between operations  0.67 us (2%)
    pallas_call x1, Pallas kernels, on_device(): pl.pallas_call(functools.partial(kernel, heads_count), out_shape=(sds((ro...  20.3 us
    unnamed x30, local copies, waits for them, and re-layouts  13.7 us

profile of v1, /device:TPU:0, one launch (start us, length us, event | category | flops | bytes accessed | tf_op | source)
XLA Modules:
  0.0 34.6 jit_solution(6551650553902092562)
XLA Ops:
  0.6 0.0 copy-start
  0.6 1.6 %copy-done = bf16[4,16,64,256]{3,2,1,0:T(8,128)(2,1)S(1)} copy-done((bf16[4,16,64,256]{3,2,1,0:T(8,128)(2,1)S(1)}, bf16[4,16,64,256]{3,2,1,0:T(8,128)(2,1)}, u32[]{:S(2)}) %copy-start) | copy-done | bytes 2097176
  2.2 0.0 copy-start.1
  2.2 1.2 %copy-done.1 = bf16[4096,128]{1,0:T(8,128)(2,1)S(1)} copy-done((bf16[4096,128]{1,0:T(8,128)(2,1)S(1)}, bf16[4096,128]{1,0:T(8,128)(2,1)}, u32[]{:S(2)}) %copy-start.1) | copy-done | bytes 1048600
  3.5 0.0 copy-start.2
  3.5 0.9 %copy-done.2 = bf16[4096,16]{0,1:T(8,128)(2,1)S(1)} copy-done((bf16[4096,16]{0,1:T(8,128)(2,1)S(1)}, bf16[4096,16]{0,1:T(8,128)(2,1)}, u32[]{:S(2)}) %copy-start.2) | copy-done | bytes 131096
  4.4 0.0 copy-start.3
  4.4 0.8 %copy-done.3 = bf16[4,4096]{1,0:T(4,128)(2,1)S(1)} copy-done((bf16[4,4096]{1,0:T(4,128)(2,1)S(1)}, bf16[4,4096]{1,0:T(4,128)(2,1)}, u32[]{:S(2)}) %copy-start.3) | copy-done | bytes 32792
  5.1 0.0 copy-start.4
  5.1 0.7 %copy-done.4 = bf16[4,3,1024]{2,0,1:T(4,128)(2,1)S(1)} copy-done((bf16[4,3,1024]{2,0,1:T(4,128)(2,1)S(1)}, bf16[4,3,1024]{2,0,1:T(4,128)(2,1)}, u32[]{:S(2)}) %copy-start.4) | copy-done | bytes 24600
  5.9 0.0 copy-start.5
  5.9 0.7 %copy-done.5 = bf16[4,1024]{1,0:T(4,128)(2,1)S(1)} copy-done((bf16[4,1024]{1,0:T(4,128)(2,1)S(1)}, bf16[4,1024]{1,0:T(4,128)(2,1)}, u32[]{:S(2)}) %copy-start.5) | copy-done | bytes 8216
  6.6 0.0 copy-start.6
  6.6 0.7 %copy-done.6 = f32[1024]{0:T(1024)S(1)} copy-done((f32[1024]{0:T(1024)S(1)}, f32[1024]{0:T(1024)}, u32[]{:S(2)}) %copy-start.6) | copy-done | bytes 4120
  7.2 0.0 copy-start.7
  7.2 0.7 %copy-done.7 = bf16[4,3,128]{2,0,1:T(4,128)(2,1)S(1)} copy-done((bf16[4,3,128]{2,0,1:T(4,128)(2,1)S(1)}, bf16[4,3,128]{2,0,1:T(4,128)(2,1)}, u32[]{:S(2)}) %copy-start.7) | copy-done | bytes 3096
  7.9 0.0 copy-start.8
  7.9 0.7 %copy-done.8 = bf16[4,128]{1,0:T(4,128)(2,1)S(1)} copy-done((bf16[4,128]{1,0:T(4,128)(2,1)S(1)}, bf16[4,128]{1,0:T(4,128)(2,1)}, u32[]{:S(2)}) %copy-start.8) | copy-done | bytes 1048
  8.6 0.0 copy-start.9
  8.6 0.7 %copy-done.9 = s32[16]{0:T(128)S(1)} copy-done((s32[16]{0:T(128)S(1)}, s32[16]{0:T(128)}, u32[]{:S(2)}) %copy-start.9) | copy-done | bytes 88
  9.3 0.0 copy-start.10
  9.3 0.7 %copy-done.10 = f32[16]{0:T(128)S(1)} copy-done((f32[16]{0:T(128)S(1)}, f32[16]{0:T(128)}, u32[]{:S(2)}) %copy-start.10) | copy-done | bytes 88
  9.9 0.0 copy-start.11
  9.9 0.7 %copy-done.11 = f32[16]{0:T(128)S(1)} copy-done((f32[16]{0:T(128)S(1)}, f32[16]{0:T(128)}, u32[]{:S(2)}) %copy-start.11) | copy-done | bytes 88
  10.6 0.0 copy-start.12
  10.6 0.7 %copy-done.12 = f32[16]{0:T(128)S(1)} copy-done((f32[16]{0:T(128)S(1)}, f32[16]{0:T(128)}, u32[]{:S(2)}) %copy-start.12) | copy-done | bytes 88
  11.2 20.3 %shard_map.183 = (bf16[4,1024]{1,0:T(4,128)(2,1)S(1)}, bf16[4,16,64,256]{3,2,1,0:T(8,128)(2,1)S(1)}, bf16[3,4,1024]{2,1,0:T(4,128)(2,1)S(1)}, bf16[3,4,128]{2,1,0:T(4,128)(2,1)S(1)}) custom-call(bf16[4,4096]{1,0:T(4,128)(2,1)S(1)} %copy-done.3, s32[16]{0:T(128)S(1)} %copy-done.9, bf16[4,16,64,256]{3,2,1,0:T(8,128)(2,1)S(1)} %copy-done, ...), custom_call_target="tpu_custom_call" | custom-call | tf_op jit(solution)/shard_map/pallas_call | solution.py:316
  31.5 0.6 %copy.24 = bf16[4,1024]{1,0:T(4,128)(2,1)} copy(bf16[4,1024]{1,0:T(4,128)(2,1)S(1)} %get-tuple-element.16) | data formatting | bytes 16384
  32.1 1.3 %copy.25 = bf16[4,16,64,256]{3,2,1,0:T(8,128)(2,1)} copy(bf16[4,16,64,256]{3,2,1,0:T(8,128)(2,1)S(1)} %get-tuple-element.17) | data formatting | bytes 4194304
  33.5 0.6 %copy.26 = bf16[4,3,1024]{2,0,1:T(4,128)(2,1)} copy(bf16[4,3,1024]{2,0,1:T(4,128)(2,1)S(1)} %bitcast.11) | data formatting | bytes 49152
  34.1 0.6 %copy.27 = bf16[4,3,128]{2,0,1:T(4,128)(2,1)} copy(bf16[4,3,128]{2,0,1:T(4,128)(2,1)S(1)} %bitcast.14) | data formatting | bytes 6144
Async XLA Ops:
  0.6 1.6 %copy-start = (bf16[4,16,64,256]{3,2,1,0:T(8,128)(2,1)S(1)}, bf16[4,16,64,256]{3,2,1,0:T(8,128)(2,1)}, u32[]{:S(2)}) copy-start(bf16[4,16,64,256]{3,2,1,0:T(8,128)(2,1)} %ssm_state.1) | copy-start | bytes 6291460
  2.2 1.2 %copy-start.1 = (bf16[4096,128]{1,0:T(8,128)(2,1)S(1)}, bf16[4096,128]{1,0:T(8,128)(2,1)}, u32[]{:S(2)}) copy-start(bf16[4096,128]{1,0:T(8,128)(2,1)} %w_bc.1) | copy-start | bytes 3145732
  3.5 0.9 %copy-start.2 = (bf16[4096,16]{0,1:T(8,128)(2,1)S(1)}, bf16[4096,16]{0,1:T(8,128)(2,1)}, u32[]{:S(2)}) copy-start(bf16[4096,16]{0,1:T(8,128)(2,1)} %param.24) | copy-start | bytes 393220
  4.4 0.8 %copy-start.3 = (bf16[4,4096]{1,0:T(4,128)(2,1)S(1)}, bf16[4,4096]{1,0:T(4,128)(2,1)}, u32[]{:S(2)}) copy-start(bf16[4,4096]{1,0:T(4,128)(2,1)} %hidden.1) | copy-start | bytes 98308
  5.1 0.7 %copy-start.4 = (bf16[4,3,1024]{2,0,1:T(4,128)(2,1)S(1)}, bf16[4,3,1024]{2,0,1:T(4,128)(2,1)}, u32[]{:S(2)}) copy-start(bf16[4,3,1024]{2,0,1:T(4,128)(2,1)} %param.19) | copy-start | bytes 73732
  5.9 0.7 %copy-start.5 = (bf16[4,1024]{1,0:T(4,128)(2,1)S(1)}, bf16[4,1024]{1,0:T(4,128)(2,1)}, u32[]{:S(2)}) copy-start(bf16[4,1024]{1,0:T(4,128)(2,1)} %conv_wx.1) | copy-start | bytes 24580
  6.6 0.7 %copy-start.6 = (f32[1024]{0:T(1024)S(1)}, f32[1024]{0:T(1024)}, u32[]{:S(2)}) copy-start(f32[1024]{0:T(1024)} %param.30) | copy-start | bytes 12292
  7.2 0.7 %copy-start.7 = (bf16[4,3,128]{2,0,1:T(4,128)(2,1)S(1)}, bf16[4,3,128]{2,0,1:T(4,128)(2,1)}, u32[]{:S(2)}) copy-start(bf16[4,3,128]{2,0,1:T(4,128)(2,1)} %param.20) | copy-start | bytes 9220
  7.9 0.7 %copy-start.8 = (bf16[4,128]{1,0:T(4,128)(2,1)S(1)}, bf16[4,128]{1,0:T(4,128)(2,1)}, u32[]{:S(2)}) copy-start(bf16[4,128]{1,0:T(4,128)(2,1)} %conv_wbc.1) | copy-start | bytes 3076
  8.6 0.7 %copy-start.9 = (s32[16]{0:T(128)S(1)}, s32[16]{0:T(128)}, u32[]{:S(2)}) copy-start(s32[16]{0:T(128)} %parent.1) | copy-start | bytes 196
  9.3 0.7 %copy-start.10 = (f32[16]{0:T(128)S(1)}, f32[16]{0:T(128)}, u32[]{:S(2)}) copy-start(f32[16]{0:T(128)} %param.25) | copy-start | bytes 196
  9.9 0.7 %copy-start.11 = (f32[16]{0:T(128)S(1)}, f32[16]{0:T(128)}, u32[]{:S(2)}) copy-start(f32[16]{0:T(128)} %param.26) | copy-start | bytes 196
  10.6 0.7 %copy-start.12 = (f32[16]{0:T(128)S(1)}, f32[16]{0:T(128)}, u32[]{:S(2)}) copy-start(f32[16]{0:T(128)} %param.27) | copy-start | bytes 196

commit v2 on v1

--- a/solution.py
+++ b/solution.py
@@ -22,14 +22,29 @@
 
 def kernel(
     heads_count,
-    hidden,
-    parent,
+    hidden_hbm,
+    parent_hbm,
     ssm_state,
-    conv_x,
-    conv_bc,
+    conv_x_hbm,
+    conv_bc_hbm,
     w_gate,
     w_x,
     w_bc,
+    w_dt_hbm,
+    dt_bias_hbm,
+    a_log_hbm,
+    d_skip_hbm,
+    conv_wx_hbm,
+    conv_wbc_hbm,
+    norm_gain_hbm,
+    w_out,
+    mixed,
+    new_state,
+    new_cx,
+    new_cbc,
+    hidden,
+    conv_x,
+    conv_bc,
     w_dt,
     dt_bias,
     a_log,
@@ -37,11 +52,8 @@
     conv_wx,
     conv_wbc,
     norm_gain,
-    w_out,
-    mixed,
-    new_state,
-    new_cx,
-    new_cbc,
+    parent,
+    in_sem,
     wbc_v,
     wx_v,
     wg_v,
@@ -94,8 +106,26 @@
         at = pl.ds(pl.multiple_of(p * out_cols, out_cols), out_cols)
         return pltpu.make_async_copy(w_out.at[:, at], wo_v.at[step], o_sem.at[step])
 
+    small = (
+        (hidden_hbm, hidden),
+        (conv_x_hbm, conv_x),
+        (conv_bc_hbm, conv_bc),
+        (w_dt_hbm, w_dt),
+        (dt_bias_hbm, dt_bias),
+        (a_log_hbm, a_log),
+        (d_skip_hbm, d_skip),
+        (conv_wx_hbm, conv_wx),
+        (conv_wbc_hbm, conv_wbc),
+        (norm_gain_hbm, norm_gain),
+        (parent_hbm, parent),
+    )
+    loads = [pltpu.make_async_copy(a, b, in_sem.at[i]) for i, (a, b) in enumerate(small)]
     wbc_copy = pltpu.make_async_copy(w_bc, wbc_v, bc_sem)
+    for i in (1, 2, 0):
+        loads[i].start()
     wbc_copy.start()
+    for i in range(3, len(loads)):
+        loads[i].start()
     for k in range(CHUNKS):
         chunk_copy(w_x, wx_v, x_sem, k).start()
     own_state = pltpu.make_async_copy(ssm_state, st_all.at[mine], st_sem)
@@ -111,6 +141,8 @@
     for step in range(1, heads_count):
         pl.semaphore_signal(barrier, inc=1, device_id={"heads": peer(step)}, device_id_type=MESH)
 
+    loads[1].wait()
+    loads[2].wait()
     for r in range(rows_dev):
         for k in range(taps - 1):
             win_all[member * rows_dev + r, k : k + 1, :inner] = conv_x[k, r : r + 1, :].astype(F32)
@@ -137,6 +169,9 @@
     )
     state_copy.start()
 
+    loads[0].wait()
+    for load in loads[3:]:
+        load.wait()
     dt_raw = lax.dot_general(hidden[...], w_dt[...], NT, preferred_element_type=F32)
     wbc_copy.wait()
     bcin = jnp.dot(hidden[...], wbc_v[...], preferred_element_type=F32).astype(BF16).astype(F32)
@@ -281,6 +316,15 @@
         rs_copy(step, me).wait_send()
     for r in range(rows_dev):
         pltpu.make_async_copy(ns_v.at[r], new_state.at[r], ns_sem.at[r]).wait()
+
+
+def store_kernel(*refs):
+    sem = refs[8]
+    copies = [pltpu.make_async_copy(refs[i], refs[4 + i], sem.at[i]) for i in (1, 0, 2, 3)]
+    for copy in copies:
+        copy.start()
+    for copy in copies:
+        copy.wait()
 
 
 def on_device(
@@ -309,11 +353,10 @@
     taps = conv_wx.shape[0]
     out_cols = w_out.shape[1] // heads_count
     vmem = pl.BlockSpec(memory_space=pltpu.VMEM)
-    smem = pl.BlockSpec(memory_space=pltpu.SMEM)
-    hbm = pl.BlockSpec(memory_space=pl.ANY)
+    hbm = pl.BlockSpec(memory_space=pltpu.HBM)
     dma = pltpu.SemaphoreType.DMA
     sds = jax.ShapeDtypeStruct
-    mixed, new_state, new_cx, new_cbc = pl.pallas_call(
+    results = pl.pallas_call(
         functools.partial(kernel, heads_count),
         out_shape=(
             sds((rows_dev, out_cols), BF16),
@@ -321,9 +364,21 @@
             sds((taps - 1, rows_dev, inner), BF16),
             sds((taps - 1, rows_dev, bcw), BF16),
         ),
-        in_specs=[vmem, smem, hbm, vmem, vmem, hbm, hbm, hbm] + [vmem] * 7 + [hbm],
+        in_specs=[hbm] * 16,
         out_specs=(vmem, hbm, vmem, vmem),
         scratch_shapes=[
+            pltpu.VMEM(hidden.shape, BF16),
+            pltpu.VMEM((taps - 1, rows_dev, inner), BF16),
+            pltpu.VMEM((taps - 1, rows_dev, bcw), BF16),
+            pltpu.VMEM((heads_dev, depth), BF16),
+            pltpu.VMEM((1, heads_dev), F32),
+            pltpu.VMEM((1, heads_dev), F32),
+            pltpu.VMEM((1, heads_dev), F32),
+            pltpu.VMEM(conv_wx.shape, BF16),
+            pltpu.VMEM(conv_wbc.shape, BF16),
+            pltpu.VMEM((1, inner), F32),
+            pltpu.SMEM(parent.shape, jnp.int32),
+            dma((11,)),
             pltpu.VMEM((depth, bcw), BF16),
             pltpu.VMEM((depth, inner), BF16),
             pltpu.VMEM((depth, inner), BF16),
@@ -350,7 +405,7 @@
             dma((heads_count,)),
         ],
         compiler_params=pltpu.CompilerParams(
-            collective_id=0, has_side_effects=True, vmem_limit_bytes=48 * 1024 * 1024
+            collective_id=0, has_side_effects=True, vmem_limit_bytes=60 * 1024 * 1024
         ),
     )(
         hidden,
@@ -370,6 +425,13 @@
         norm_gain.reshape(1, -1),
         w_out,
     )
+    mixed, new_state, new_cx, new_cbc = pl.pallas_call(
+        store_kernel,
+        out_shape=tuple(sds(v.shape, v.dtype) for v in results),
+        in_specs=[pl.BlockSpec(memory_space=pl.ANY)] * 4,
+        out_specs=(hbm,) * 4,
+        scratch_shapes=[dma((4,))],
+    )(*results)
     return (
         mixed,
         new_state,

time: 35.1 us -> 90.9 us (2.59)
  Pallas kernels: 20.3 us -> 90.1 us
  local copies, waits for them, and re-layouts: 13.7 us -> 0 us
    pallas_call x0 -> x1, Pallas kernels: none -> 65.8 us  [on_device(): pl.pallas_call(store_kernel, out_shape=tuple((sds(v.shape, v.dtype) for v...]
    unnamed x30 -> x0, local copies, waits for them, and re-layouts: 13.7 us -> none
    pallas_call x1, Pallas kernels: 20.3 us -> 24.3 us  [on_device(): pl.pallas_call(functools.partial(kernel, heads_count), out_shape=(sds((ro...]
where the time goes in v2:
time: 90.9 us; the launch traced here: 90.7 us
  Pallas kernels  90.1 us (99%)
    pallas_call x1, Pallas kernels, on_device(): pl.pallas_call(store_kernel, out_shape=tuple((sds(v.shape, v.dtype) for v...  65.8 us
    pallas_call x1, Pallas kernels, on_device(): pl.pallas_call(functools.partial(kernel, heads_count), out_shape=(sds((ro...  24.3 us

profile of v2, /device:TPU:0, one launch (start us, length us, event | category | flops | bytes accessed | tf_op | source)
XLA Modules:
  0.0 90.7 jit_solution(2035746293927946322)
XLA Ops:
  0.6 24.3 %shard_map.183 = (bf16[4,1024]{1,0:T(4,128)(2,1)}, bf16[4,16,64,256]{3,2,1,0:T(8,128)(2,1)}, bf16[3,4,1024]{2,1,0:T(4,128)(2,1)}, bf16[3,4,128]{2,1,0:T(4,128)(2,1)}) custom-call(bf16[4,4096]{1,0:T(4,128)(2,1)} %hidden_hbm.1, s32[16]{0:T(128)} %parent_hbm.1, bf16[4,16,64,256]{3,2,1,0:T(8,128)(2,1)} %ssm_state.1, bf16[3,4,1024]{2,1,0:T(4,128)(2,1)} %bitcast.10, ...), custom_call_target="tpu_custom_call" | custom-call | tf_op jit(solution)/shard_map/pallas_call | solution.py:359
  25.0 65.8 %shard_map.184 = (bf16[4,1024]{1,0:T(4,128)(2,1)}, bf16[4,16,64,256]{3,2,1,0:T(8,128)(2,1)}, bf16[3,4,1024]{2,1,0:T(4,128)(2,1)}, bf16[3,4,128]{2,1,0:T(4,128)(2,1)}) custom-call(bf16[4,1024]{1,0:T(4,128)(2,1)} %get-tuple-element.12.refs_0_, bf16[4,16,64,256]{3,2,1,0:T(8,128)(2,1)} %get-tuple-element.13.refs_1_, ...), custom_call_target="tpu_custom_call" | custom-call | tf_op jit(solution)/shard_map/pallas_call | solution.py:428

commit v3 on v2

--- a/solution.py
+++ b/solution.py
@@ -319,12 +319,21 @@
 
 
 def store_kernel(*refs):
-    sem = refs[8]
-    copies = [pltpu.make_async_copy(refs[i], refs[4 + i], sem.at[i]) for i in (1, 0, 2, 3)]
-    for copy in copies:
-        copy.start()
-    for copy in copies:
-        copy.wait()
+    ins, outs, held = refs[:4], refs[4:8], refs[8:12]
+    in_sem, out_sem = refs[12:]
+    rows_dev = ins[1].shape[0]
+    loads = [pltpu.make_async_copy(ins[1].at[r], held[1].at[r], in_sem.at[r]) for r in range(rows_dev)]
+    stores = [pltpu.make_async_copy(held[1].at[r], outs[1].at[r], out_sem.at[r]) for r in range(rows_dev)]
+    for n, i in enumerate((0, 2, 3)):
+        loads.append(pltpu.make_async_copy(ins[i], held[i], in_sem.at[rows_dev + n]))
+        stores.append(pltpu.make_async_copy(held[i], outs[i], out_sem.at[rows_dev + n]))
+    for load in loads:
+        load.start()
+    for load, store in zip(loads, stores):
+        load.wait()
+        store.start()
+    for store in stores:
+        store.wait()
 
 
 def on_device(
@@ -428,9 +437,11 @@
     mixed, new_state, new_cx, new_cbc = pl.pallas_call(
         store_kernel,
         out_shape=tuple(sds(v.shape, v.dtype) for v in results),
-        in_specs=[pl.BlockSpec(memory_space=pl.ANY)] * 4,
+        in_specs=[hbm] * 4,
         out_specs=(hbm,) * 4,
-        scratch_shapes=[dma((4,))],
+        scratch_shapes=[pltpu.VMEM(v.shape, v.dtype) for v in results]
+        + [dma((rows_dev + 3,)), dma((rows_dev + 3,))],
+        compiler_params=pltpu.CompilerParams(vmem_limit_bytes=60 * 1024 * 1024),
     )(*results)
     return (
         mixed,

time: 90.9 us -> 27.6 us (0.30)
  Pallas kernels: 90.1 us -> 26.8 us
    pallas_call x1, Pallas kernels: 65.8 us -> 2.48 us  [on_device(): pl.pallas_call(store_kernel, out_shape=tuple((sds(v.shape, v.dtype) for v...]
where the time goes in v3:
time: 27.6 us; the launch traced here: 27.4 us
  Pallas kernels  26.8 us (97%)
  between operations  0.65 us (2%)
    pallas_call x1, Pallas kernels, on_device(): pl.pallas_call(functools.partial(kernel, heads_count), out_shape=(sds((ro...  24.3 us
    pallas_call x1, Pallas kernels, on_device(): pl.pallas_call(store_kernel, out_shape=tuple((sds(v.shape, v.dtype) for v...  2.48 us

profile of v3, /device:TPU:0, one launch (start us, length us, event | category | flops | bytes accessed | tf_op | source)
XLA Modules:
  0.0 27.4 jit_solution(8514320699250734782)
XLA Ops:
  0.6 24.3 %shard_map.183 = (bf16[4,1024]{1,0:T(4,128)(2,1)}, bf16[4,16,64,256]{3,2,1,0:T(8,128)(2,1)}, bf16[3,4,1024]{2,1,0:T(4,128)(2,1)}, bf16[3,4,128]{2,1,0:T(4,128)(2,1)}) custom-call(bf16[4,4096]{1,0:T(4,128)(2,1)} %hidden_hbm.1, s32[16]{0:T(128)} %parent_hbm.1, bf16[4,16,64,256]{3,2,1,0:T(8,128)(2,1)} %ssm_state.1, bf16[3,4,1024]{2,1,0:T(4,128)(2,1)} %bitcast.10, ...), custom_call_target="tpu_custom_call" | custom-call | tf_op jit(solution)/shard_map/pallas_call | solution.py:368
  25.0 2.5 %shard_map.184 = (bf16[4,1024]{1,0:T(4,128)(2,1)}, bf16[4,16,64,256]{3,2,1,0:T(8,128)(2,1)}, bf16[3,4,1024]{2,1,0:T(4,128)(2,1)}, bf16[3,4,128]{2,1,0:T(4,128)(2,1)}) custom-call(bf16[4,1024]{1,0:T(4,128)(2,1)} %get-tuple-element.12.refs_0_, bf16[4,16,64,256]{3,2,1,0:T(8,128)(2,1)} %get-tuple-element.13.refs_1_, ...), custom_call_target="tpu_custom_call" | custom-call | tf_op jit(solution)/shard_map/pallas_call | solution.py:437

commit v4 on v3

--- a/solution.py
+++ b/solution.py
@@ -130,11 +130,7 @@
         chunk_copy(w_x, wx_v, x_sem, k).start()
     own_state = pltpu.make_async_copy(ssm_state, st_all.at[mine], st_sem)
     own_state.start()
-    for k in range(CHUNKS):
-        chunk_copy(w_gate, wg_v, g_sem, k).start()
     out_order = list(range(1, heads_count)) + [0]
-    for step in out_order:
-        out_copy(step).start()
 
     barrier = pltpu.get_barrier_semaphore()
     pl.semaphore_signal(barrier, inc=1, device_id={"rows": partner}, device_id_type=MESH)
@@ -168,6 +164,10 @@
         device_id_type=MESH,
     )
     state_copy.start()
+    for k in range(CHUNKS):
+        chunk_copy(w_gate, wg_v, g_sem, k).start()
+    for step in out_order:
+        out_copy(step).start()
 
     loads[0].wait()
     for load in loads[3:]:
@@ -234,8 +234,6 @@
     pushed = per_column(dt) * xconv
     skip_c = per_column(d_skip[...])
     cols_t[...] = jnp.transpose(jnp.concatenate([pushed, decay_c], axis=0))
-
-    gate = project(w_gate, wg_v, g_sem)
 
     for step in range(1, heads_count):
         bc_copy(step, peer(step)).wait_recv()
@@ -266,6 +264,25 @@
         seen = lax.dot_general(cmap_b, block, NT, preferred_element_type=F32)
         carried = jnp.where(row_of == r, seen, carried)
     overlap = jnp.sum(bmap * cmap, axis=1, keepdims=True)
+
+    def update_rows(first, last):
+        for r in range(first, last):
+            b_row = bmap[r : r + 1, :]
+
+            def one_head(h, carry, r=r, b_row=b_row):
+                at = pl.ds(pl.multiple_of(h * head_dim, head_dim), head_dim)
+                cols = cols_t[at, :]
+                prior = st_all[sources[r], h].astype(F32)
+                value = cols[:, rows_dev + r : rows_dev + r + 1] * prior + cols[:, r : r + 1] * b_row
+                ns_v[r, h] = value.astype(BF16)
+                return carry
+
+            lax.fori_loop(0, heads_dev, one_head, 0, unroll=2)
+            pltpu.make_async_copy(ns_v.at[r], new_state.at[r], ns_sem.at[r]).start()
+
+    early = rows_dev // 2
+    update_rows(0, early)
+    gate = project(w_gate, wg_v, g_sem)
     y = decay_c * carried + pushed * overlap + skip_c * xconv
     gated = y * silu(gate)
     squares = jnp.sum(gated * gated, axis=1, keepdims=True)
@@ -290,19 +307,7 @@
         if step > 0:
             rs_copy(step, me).start()
 
-    for r in range(rows_dev):
-        b_row = bmap[r : r + 1, :]
-
-        def one_head(h, carry, r=r, b_row=b_row):
-            at = pl.ds(pl.multiple_of(h * head_dim, head_dim), head_dim)
-            cols = cols_t[at, :]
-            prior = st_all[sources[r], h].astype(F32)
-            value = cols[:, rows_dev + r : rows_dev + r + 1] * prior + cols[:, r : r + 1] * b_row
-            ns_v[r, h] = value.astype(BF16)
-            return carry
-
-        lax.fori_loop(0, heads_dev, one_head, 0)
-        pltpu.make_async_copy(ns_v.at[r], new_state.at[r], ns_sem.at[r]).start()
+    update_rows(early, rows_dev)
 
     total = rs_send[0]
     for step in range(1, heads_count):

time: 27.6 us -> 23.5 us (0.85)
  Pallas kernels: 26.8 us -> 22.7 us
    pallas_call x1, Pallas kernels: 24.3 us -> 20.2 us  [on_device(): pl.pallas_call(functools.partial(kernel, heads_count), out_shape=(sds((ro...]
where the time goes in v4:
time: 23.5 us; the launch traced here: 23.4 us
  Pallas kernels  22.7 us (97%)
  between operations  0.65 us (3%)
    pallas_call x1, Pallas kernels, on_device(): pl.pallas_call(functools.partial(kernel, heads_count), out_shape=(sds((ro...  20.2 us
    pallas_call x1, Pallas kernels, on_device(): pl.pallas_call(store_kernel, out_shape=tuple((sds(v.shape, v.dtype) for v...  2.48 us

profile of v4, /device:TPU:0, one launch (start us, length us, event | category | flops | bytes accessed | tf_op | source)
XLA Modules:
  0.0 23.4 jit_solution(10965147429482724481)
XLA Ops:
  0.6 20.2 %shard_map.183 = (bf16[4,1024]{1,0:T(4,128)(2,1)}, bf16[4,16,64,256]{3,2,1,0:T(8,128)(2,1)}, bf16[3,4,1024]{2,1,0:T(4,128)(2,1)}, bf16[3,4,128]{2,1,0:T(4,128)(2,1)}) custom-call(bf16[4,4096]{1,0:T(4,128)(2,1)} %hidden_hbm.1, s32[16]{0:T(128)} %parent_hbm.1, bf16[4,16,64,256]{3,2,1,0:T(8,128)(2,1)} %ssm_state.1, bf16[3,4,1024]{2,1,0:T(4,128)(2,1)} %bitcast.10, ...), custom_call_target="tpu_custom_call" | custom-call | tf_op jit(solution)/shard_map/pallas_call | solution.py:373
  20.9 2.5 %shard_map.184 = (bf16[4,1024]{1,0:T(4,128)(2,1)}, bf16[4,16,64,256]{3,2,1,0:T(8,128)(2,1)}, bf16[3,4,1024]{2,1,0:T(4,128)(2,1)}, bf16[3,4,128]{2,1,0:T(4,128)(2,1)}) custom-call(bf16[4,1024]{1,0:T(4,128)(2,1)} %get-tuple-element.12.refs_0_, bf16[4,16,64,256]{3,2,1,0:T(8,128)(2,1)} %get-tuple-element.13.refs_1_, ...), custom_call_target="tpu_custom_call" | custom-call | tf_op jit(solution)/shard_map/pallas_call | solution.py:442

commit v5 on v4

--- a/solution.py
+++ b/solution.py
@@ -126,10 +126,7 @@
     wbc_copy.start()
     for i in range(3, len(loads)):
         loads[i].start()
-    for k in range(CHUNKS):
-        chunk_copy(w_x, wx_v, x_sem, k).start()
     own_state = pltpu.make_async_copy(ssm_state, st_all.at[mine], st_sem)
-    own_state.start()
     out_order = list(range(1, heads_count)) + [0]
 
     barrier = pltpu.get_barrier_semaphore()
@@ -163,6 +160,9 @@
         device_id={"rows": partner},
         device_id_type=MESH,
     )
+    for k in range(CHUNKS):
+        chunk_copy(w_x, wx_v, x_sem, k).start()
+    own_state.start()
     state_copy.start()
     for k in range(CHUNKS):
         chunk_copy(w_gate, wg_v, g_sem, k).start()

time: 23.5 us -> 22.8 us (0.970)
  Pallas kernels: 22.7 us -> 21.9 us
    pallas_call x1, Pallas kernels: 20.2 us -> 19.5 us  [on_device(): pl.pallas_call(functools.partial(kernel, heads_count), out_shape=(sds((ro...]
where the time goes in v5:
time: 22.8 us; the launch traced here: 22.6 us
  Pallas kernels  21.9 us (96%)
  between operations  0.65 us (3%)
    pallas_call x1, Pallas kernels, on_device(): pl.pallas_call(functools.partial(kernel, heads_count), out_shape=(sds((ro...  19.5 us
    pallas_call x1, Pallas kernels, on_device(): pl.pallas_call(store_kernel, out_shape=tuple((sds(v.shape, v.dtype) for v...  2.48 us

profile of v5, /device:TPU:0, one launch (start us, length us, event | category | flops | bytes accessed | tf_op | source)
XLA Modules:
  0.0 22.6 jit_solution(13144508368591195342)
XLA Ops:
  0.6 19.5 %shard_map.183 = (bf16[4,1024]{1,0:T(4,128)(2,1)}, bf16[4,16,64,256]{3,2,1,0:T(8,128)(2,1)}, bf16[3,4,1024]{2,1,0:T(4,128)(2,1)}, bf16[3,4,128]{2,1,0:T(4,128)(2,1)}) custom-call(bf16[4,4096]{1,0:T(4,128)(2,1)} %hidden_hbm.1, s32[16]{0:T(128)} %parent_hbm.1, bf16[4,16,64,256]{3,2,1,0:T(8,128)(2,1)} %ssm_state.1, bf16[3,4,1024]{2,1,0:T(4,128)(2,1)} %bitcast.10, ...), custom_call_target="tpu_custom_call" | custom-call | tf_op jit(solution)/shard_map/pallas_call | solution.py:373
  20.1 2.5 %shard_map.184 = (bf16[4,1024]{1,0:T(4,128)(2,1)}, bf16[4,16,64,256]{3,2,1,0:T(8,128)(2,1)}, bf16[3,4,1024]{2,1,0:T(4,128)(2,1)}, bf16[3,4,128]{2,1,0:T(4,128)(2,1)}) custom-call(bf16[4,1024]{1,0:T(4,128)(2,1)} %get-tuple-element.12.refs_0_, bf16[4,16,64,256]{3,2,1,0:T(8,128)(2,1)} %get-tuple-element.13.refs_1_, ...), custom_call_target="tpu_custom_call" | custom-call | tf_op jit(solution)/shard_map/pallas_call | solution.py:442
